TPU v7x, 128 devices: a whole 4x4x4 slice. The times are simulated.
128 devices in a mesh: item: 32 (over z, x, core), dim: 4 (over y).
Axes of the slice: x: 4, y: 4, z: 4, core: 2. Of those that a mesh axis runs over, the one named last changes fastest.
Arguments:
- embeddings: float32 [131072, 512], P('item', 'dim'), as said below
- cand_index: int32 [3, 1024], P(None, 'item'), may hold values from 0 to 4095
- cand_count: int32 [3, 32], replicated, may hold values from 1 to 32, 512 in all within a row
Outputs:
- weights: float32 [3, 131072], P(None, ('item', 'dim'))
Inputs may be any that keep to these rules, and one draw needn't show every extreme that they name: `cand_index`: row numbers within one index of item's own 4096 rows; unused slots also hold such numbers. `cand_count`: in every round the counts add up to 512 and the largest is exactly 32. `embeddings`: finite values.
All inputs are finite; a program needn't handle non-finite values.
Results may differ from a plain program's by a relative error of at most 0.00018.
Values sent between devices are 32-bit elements; how exact they have to be, the bound alone decides.
A program may use at most 192 MiB of HBM per device.

v0:
```python
import itertools

import jax
import jax.numpy as jnp
from jax import lax
from jax.experimental import pallas as pl
from jax.experimental.pallas import tpu as pltpu
from jax.sharding import PartitionSpec as P

CAP = 4.0
MESH = pl.DeviceIdType.MESH
ROUNDS = 3
SLOTS = 32
LANES = 128
ITEMS = 32
ROWS = 4096
SHARE = 1024
STEP = 256
PIECES = SHARE // STEP
WIDE = 512
PAIRS = SHARE // WIDE
TOTAL = 131072
TILE = 8
QUARTER = SLOTS // TILE
BLOCK = 4 * QUARTER
BUNDLE = 4 * BLOCK
HALF = 4 * BUNDLE
CORE_SLOTS = 512
BF16 = jnp.bfloat16
F32 = jnp.float32


def kernel(
    index_hbm, count_hbm, x_ref, out_ref,
    index_ref, count_ref, xv, xfull, relay_buf, cand_0, cand_1, cand_2,
    ch, cl, nrm, xh, xl, sq, low, done, part, red_line, red_plane,
    load_sem, send_sem, recv_sem, cost_sem,
):
    cand = (cand_0, cand_1, cand_2)
    item, dim = lax.axis_index("item"), lax.axis_index("dim")
    z = lax.div(item, 8)
    x = lax.div(item - z * 8, 2)
    core = item - z * 8 - x * 2

    def ring(place):
        return [place] + [jnp.where(place + k > 3, place + k - 4, place + k) for k in range(1, 4)]

    xs, ys, zs = ring(x), ring(dim), ring(z)
    sibling = item + 1 - 2 * core

    def plane(dz, dx):
        return (zs[dz] * 8 + xs[dx] * 2 + core, dim)

    def axis(k, first):
        over_x, over_z = plane(0, k)[0], plane(k, 0)[0]
        lead = 1 - core if first else core
        return (over_z + lead * (over_x - over_z), dim)

    up_a, far_a, down_a = [axis(k, True) for k in range(1, 4)]
    up_b, far_b, down_b = [axis(k, False) for k in range(1, 4)]
    up_y, far_y, down_y = [(item, ys[k]) for k in range(1, 4)]
    _, y_up, y_far, y_down = ys
    line_devices = [(sibling, dim)]
    for k in range(1, 4):
        line_devices += [(item, ys[k]), (sibling, ys[k])]
    plane_devices = [plane(dz, dx) for dz in range(4) for dx in range(4) if dz or dx]

    loads = [
        pltpu.make_async_copy(index_hbm, index_ref, load_sem.at[0]),
        pltpu.make_async_copy(x_ref, xv, load_sem.at[1]),
        pltpu.make_async_copy(count_hbm, count_ref, load_sem.at[2]),
        pltpu.make_async_copy(x_ref.at[pl.ds(dim * SHARE, SHARE)], xfull.at[dim], load_sem.at[3]),
    ]
    for copy in loads:
        copy.start()
    index_load, x_load, count_load, own_rows = loads

    barrier = pltpu.get_barrier_semaphore()
    for target in line_devices + plane_devices:
        pl.semaphore_signal(barrier, inc=1, device_id=target, device_id_type=MESH)

    index_load.wait()
    count_load.wait()
    x_load.wait()
    pl.semaphore_wait(barrier, REDUCES)

    number = itertools.count()

    def send(src, dst, target, group):
        k = next(number)
        copy = pltpu.make_async_remote_copy(
            src_ref=src, dst_ref=dst, send_sem=send_sem.at[group], recv_sem=recv_sem.at[k],
            device_id=target, device_id_type=MESH,
        )
        copy.start()
        return copy

    def sent(ref, group):
        pltpu.make_async_copy(ref, ref, send_sem.at[group]).wait()

    half = STEP // 2
    y_copies, first, second, passes, swap, relay, near, passed = [{} for _ in range(8)]

    def near_send(t):
        lands = xfull.at[dim, pl.ds(t * STEP, STEP)]
        near[t] = (
            send(xv.at[pl.ds(y_up * SHARE + t * STEP, STEP)], lands, up_y, NEAR),
            send(xv.at[pl.ds(y_down * SHARE + t * STEP, STEP)], lands, down_y, NEAR),
        )

    def far_send(t):
        far = y_far * SHARE + t * STEP
        relay[t] = (
            send(xv.at[pl.ds(far, half)], relay_buf.at[0, t], up_y, RELAY),
            send(xv.at[pl.ds(far + half, half)], relay_buf.at[1, t], down_y, RELAY),
        )

    def far_pass(t):
        relay[t][0].wait_recv()
        up = send(relay_buf.at[0, t], xfull.at[y_down, pl.ds(t * STEP, half)], up_y, PASSED)
        relay[t][1].wait_recv()
        down = send(relay_buf.at[1, t], xfull.at[y_up, pl.ds(t * STEP + half, half)], down_y, PASSED)
        passed[t] = (up, down)

    def tiles(r, start, count):
        return cand[r].at[pl.ds(core * HALF + start, count)]

    def pick_send(r):
        def pick(g, carry):
            slots = [g * TILE + k for k in range(TILE)]
            slots = [jnp.where(slot < count_ref[r, item], slot, 0) for slot in slots]
            rows = [xv[pl.ds(index_ref[r, slot], 1), :] for slot in slots]
            cand[r][core * HALF + dim * QUARTER + g] = jnp.concatenate(rows, axis=0)
            return carry

        lax.fori_loop(0, QUARTER, pick, 0, unroll=True)

        ref = tiles(r, dim * QUARTER, QUARTER)
        y_copies[r] = [send(ref, ref, target, PICK + r) for target in (up_y, down_y, far_y)]

    def first_send(r):
        for copy in y_copies[r]:
            copy.wait_recv()
        block = tiles(r, 0, BLOCK)
        first[r] = [
            send(block, tiles(r, k * BLOCK, BLOCK), target, FIRST + r)
            for k, target in ((3, far_a), (1, up_a), (2, down_a))
        ]

    def second_send(r):
        for copy in first[r]:
            copy.wait_recv()
        bundle = tiles(r, 0, BUNDLE)
        second[r] = (
            send(bundle, tiles(r, BUNDLE, BUNDLE), up_b, SECOND + r),
            send(bundle, tiles(r, 2 * BUNDLE, BUNDLE), down_b, SECOND + r),
        )
        swap[r] = [send(bundle, bundle, (sibling, dim), SWAP + r)]

    def second_pass(r):
        part = 2 * BLOCK
        second[r][0].wait_recv()
        up = send(tiles(r, BUNDLE, part), tiles(r, 3 * BUNDLE, part), up_b, SECOND + r)
        second[r][1].wait_recv()
        down = send(tiles(r, 2 * BUNDLE + part, part), tiles(r, 3 * BUNDLE + part, part), down_b, SECOND + r)
        passes[r] = (up, down)
        ready = tiles(r, BUNDLE, 2 * BUNDLE)
        swap[r].append(send(ready, ready, (sibling, dim), SWAP + r))

    def second_end(r):
        for copy in passes[r]:
            copy.wait_recv()
        ready = tiles(r, 3 * BUNDLE, BUNDLE)
        swap[r].append(send(ready, ready, (sibling, dim), SWAP + r))

    def convert(r, side, bundle, count=1):
        start = (core * HALF if side == 0 else (1 - core) * HALF) + bundle * BUNDLE

        def one(step, carry):
            for k in range(4):
                at = pl.ds(pl.multiple_of(step * 4 * SLOTS + k * SLOTS, SLOTS), SLOTS)
                total = jnp.zeros((SLOTS, LANES), F32)
                for q in range(4):
                    place = start + (step - bundle) * BUNDLE + k * BLOCK + q * QUARTER
                    value = cand[r][pl.ds(place, QUARTER)].reshape(SLOTS, LANES)
                    total += value * value
                    high = value.astype(BF16)
                    ch[r, side, at, q * LANES:(q + 1) * LANES] = high
                    cl[r, side, at, q * LANES:(q + 1) * LANES] = (value - high.astype(F32)).astype(BF16)
                norm = jnp.sum(total, axis=1, keepdims=True)
                nrm[r, side, at, :] = jnp.broadcast_to(norm, (SLOTS, LANES))
            return carry

        lax.fori_loop(bundle, bundle + count, one, 0)

    def prepare(t):
        for copy in near[t] + passed[t]:
            copy.wait_recv()
        at = slice(t % 2 * STEP, (t % 2 + 1) * STEP)
        total = jnp.zeros((LANES, STEP), F32)
        for q in range(4):
            value = xfull[q, t * STEP:(t + 1) * STEP, :].T
            total += value * value
            value = -2.0 * value
            high = value.astype(BF16)
            xh[t // 2, q * LANES:(q + 1) * LANES, at] = high
            xl[t // 2, q * LANES:(q + 1) * LANES, at] = (value - high.astype(F32)).astype(BF16)
        sq[t // 2, :, at] = jnp.sum(total.reshape(LANES // 8, 8, STEP), axis=0)

    def nearest(t, r, side):
        high, rows = ch[r, side], xh[t]
        value = jnp.dot(
            jnp.concatenate([high, cl[r, side], high], axis=1),
            jnp.concatenate([rows, rows, xl[t]], axis=0),
            preferred_element_type=F32,
        )
        value = value + jnp.concatenate([nrm[r, side]] * (WIDE // LANES), axis=1)
        low[t, r, side] = jnp.min(value.reshape(CORE_SLOTS // 8, 8, WIDE), axis=0)

    def finish(t):
        norm = jnp.sum(sq[t], axis=0, keepdims=True)
        best = [
            jnp.min(jnp.minimum(low[t, r, 0], low[t, r, 1]), axis=0, keepdims=True) for r in range(ROUNDS)
        ]
        for r in range(1, ROUNDS):
            best[r] = jnp.minimum(best[r], best[r - 1])
        done[:, t * WIDE:(t + 1) * WIDE] = jnp.concatenate(
            [jnp.maximum(value + norm, 0.0) for value in best], axis=0
        )

    def many(count, body):
        def one(k, carry):
            body(k)
            return carry

        lax.fori_loop(0, count, one, 0)

    def convert_swapped(r):
        for copy in swap[r]:
            copy.wait_recv()
        convert(r, 1, 0, 4)

    pick_send(0)
    pick_send(1)
    far_send(0)
    pick_send(2)
    first_send(0)
    far_send(1)
    first_send(1)
    near_send(0)
    first_send(2)
    second_send(0)
    far_pass(0)
    convert(0, 0, 0)
    second_send(1)
    far_send(2)
    convert(1, 0, 0)
    near_send(1)
    far_send(3)
    far_pass(1)
    own_rows.wait()
    prepare(0)
    second_pass(0)
    convert(0, 0, 1, 2)
    second_send(2)
    second_pass(1)
    convert(1, 0, 1, 2)
    near_send(2)
    far_pass(2)
    second_end(0)
    far_pass(3)
    convert(0, 0, 3)
    convert(2, 0, 0)
    near_send(3)
    prepare(1)
    nearest(0, 0, 0)
    second_pass(2)
    convert(2, 0, 1, 2)
    second_end(1)
    convert_swapped(0)
    convert(1, 0, 3)
    nearest(0, 0, 1)
    second_end(2)
    nearest(0, 1, 0)
    convert(2, 0, 3)
    convert_swapped(1)
    nearest(0, 2, 0)
    nearest(0, 1, 1)
    prepare(2)
    convert_swapped(2)
    nearest(0, 2, 1)
    finish(0)
    for r in range(ROUNDS):
        sent(cand[r].at[pl.ds(0, 3 * QUARTER)], PICK + r)
        sent(cand[r].at[pl.ds(0, 3 * BLOCK)], FIRST + r)
        sent(cand[r].at[pl.ds(0, 3 * BUNDLE)], SECOND + r)
        sent(cand[r].at[pl.ds(0, HALF)], SWAP + r)
    prepare(3)
    sent(xfull.at[pl.ds(0, 1)], RELAY)
    sent(xfull.at[pl.ds(0, 2)], NEAR)
    sent(xfull.at[pl.ds(0, 1)], PASSED)
    many(2 * ROUNDS, lambda k: nearest(1, k // 2, k % 2))
    finish(1)

    sums = sum([done[:, k * LANES:(k + 1) * LANES] for k in range(SHARE // LANES)])
    line = jnp.concatenate([sums, jnp.zeros((8 - ROUNDS, LANES), F32)], axis=0)
    for stage, (targets, landed) in enumerate(((line_devices, red_line), (plane_devices, red_plane))):
        part[stage] = line
        for k, target in enumerate(targets):
            pltpu.make_async_remote_copy(
                src_ref=part.at[stage], dst_ref=landed.at[k], send_sem=send_sem.at[COST + stage],
                recv_sem=cost_sem.at[stage], device_id=target, device_id_type=MESH,
            ).start()
        pltpu.make_async_copy(landed, landed, cost_sem.at[stage]).wait()
        line = line + jnp.sum(landed[...], axis=0)
    cost = jnp.sum(line, axis=1, keepdims=True)[:ROUNDS]
    out_ref[...] = jnp.minimum(CAP, TOTAL * done[...] / cost)
    sent(red_line, COST)
    sent(red_plane, COST + 1)


COPIES = ROUNDS * 13 + PIECES * 6
REDUCES = 22
PICK, FIRST, SECOND, SWAP, RELAY, NEAR, PASSED, COST = 0, 3, 6, 9, 12, 13, 14, 15
ANY = pl.BlockSpec(memory_space=pl.ANY)


def local(embeddings, cand_index, cand_count):
    return pl.pallas_call(
        kernel,
        out_shape=jax.ShapeDtypeStruct((ROUNDS, SHARE), F32),
        in_specs=[ANY, ANY, ANY],
        out_specs=pl.BlockSpec(memory_space=pltpu.VMEM),
        scratch_shapes=[
            pltpu.SMEM((ROUNDS, SLOTS), jnp.int32),
            pltpu.SMEM((ROUNDS, ITEMS), jnp.int32),
            pltpu.VMEM((ROWS, LANES), F32),
            pltpu.VMEM((4, SHARE, LANES), F32),
            pltpu.VMEM((2, PIECES, STEP // 2, LANES), F32),
            *[pltpu.VMEM((ITEMS * BLOCK, TILE, LANES), F32)] * ROUNDS,
            pltpu.VMEM((ROUNDS, 2, CORE_SLOTS, 512), BF16),
            pltpu.VMEM((ROUNDS, 2, CORE_SLOTS, 512), BF16),
            pltpu.VMEM((ROUNDS, 2, CORE_SLOTS, LANES), F32),
            pltpu.VMEM((PAIRS, 512, WIDE), BF16),
            pltpu.VMEM((PAIRS, 512, WIDE), BF16),
            pltpu.VMEM((PAIRS, 8, WIDE), F32),
            pltpu.VMEM((PAIRS, ROUNDS, 2, 8, WIDE), F32),
            pltpu.VMEM((ROUNDS, SHARE), F32),
            pltpu.VMEM((2, 8, LANES), F32),
            pltpu.VMEM((7, 8, LANES), F32),
            pltpu.VMEM((15, 8, LANES), F32),
            pltpu.SemaphoreType.DMA((4,)),
            pltpu.SemaphoreType.DMA((COST + 2,)),
            pltpu.SemaphoreType.DMA((COPIES,)),
            pltpu.SemaphoreType.DMA((2,)),
        ],
        compiler_params=pltpu.CompilerParams(
            collective_id=0, has_side_effects=True, vmem_limit_bytes=56 * 1024 * 1024
        ),
    )(cand_index, cand_count, embeddings)


def solution(mesh):
    in_specs = (P("item", "dim"), P(None, "item"), P())
    out_specs = P(None, ("item", "dim"))
    return jax.shard_map(local, mesh=mesh, in_specs=in_specs, out_specs=out_specs, check_vma=False)
```

profile of v0, /device:TPU:1, one launch (start us, length us, event | category | flops | bytes accessed | tf_op | source)
XLA Modules:
  0.0 55.9 jit_solution(15070683066905337205)
XLA Ops:
  0.0 54.6 %shard_map.37 = f32[3,1024]{1,0:T(4,128)} custom-call(s32[3,32]{1,0:T(4,128)} %index_hbm.1, s32[3,32]{1,0:T(4,128)} %count_hbm.1, f32[4096,128]{1,0:T(8,128)} %x_ref.1), custom_call_target="tpu_custom_call" | custom-call | tf_op jit(solution)/shard_map/pallas_call | solution.py:329
  54.6 1.3 %copy.5 = f32[3,1024]{1,0:T(4,128)} copy(f32[3,1024]{1,0:T(4,128)} %shard_map.37) | data formatting | bytes 24576
where the time goes:
time: 56.1 us; the launch traced here: 55.9 us
  Pallas kernels  54.6 us (97%)
  local copies, waits for them, and re-layouts  1.33 us (2%)
    pallas_call x1, Pallas kernels, local(): pl.pallas_call(kernel, out_shape=jax.ShapeDtypeStruct((ROUNDS, SHARE), F3...  54.6 us
    unnamed x1, local copies, waits for them, and re-layouts  1.33 us

commit v1 on v0

--- a/solution.py
+++ b/solution.py
@@ -86,14 +86,20 @@
 
     number = itertools.count()
 
-    def send(src, dst, target, group):
+    def send(src, dst, target, group, like):
         k = next(number)
-        copy = pltpu.make_async_remote_copy(
+        pltpu.make_async_remote_copy(
             src_ref=src, dst_ref=dst, send_sem=send_sem.at[group], recv_sem=recv_sem.at[k],
             device_id=target, device_id_type=MESH,
-        )
-        copy.start()
-        return copy
+        ).start()
+        return lambda: pltpu.make_async_copy(like, like, recv_sem.at[k]).wait()
+
+    def send_tiles(r, start, to, count, target, group):
+        like = cand[r].at[pl.ds(0, count)]
+        return send(tiles(r, start, count), tiles(r, to, count), target, group + r, like)
+
+    def send_rows(src, dst, target, group, count):
+        return send(src, dst, target, group, xfull.at[0, pl.ds(0, count)])
 
     def sent(ref, group):
         pltpu.make_async_copy(ref, ref, send_sem.at[group]).wait()
@@ -104,22 +110,23 @@
     def near_send(t):
         lands = xfull.at[dim, pl.ds(t * STEP, STEP)]
         near[t] = (
-            send(xv.at[pl.ds(y_up * SHARE + t * STEP, STEP)], lands, up_y, NEAR),
-            send(xv.at[pl.ds(y_down * SHARE + t * STEP, STEP)], lands, down_y, NEAR),
+            send_rows(xv.at[pl.ds(y_up * SHARE + t * STEP, STEP)], lands, up_y, NEAR, STEP),
+            send_rows(xv.at[pl.ds(y_down * SHARE + t * STEP, STEP)], lands, down_y, NEAR, STEP),
         )
 
     def far_send(t):
         far = y_far * SHARE + t * STEP
         relay[t] = (
-            send(xv.at[pl.ds(far, half)], relay_buf.at[0, t], up_y, RELAY),
-            send(xv.at[pl.ds(far + half, half)], relay_buf.at[1, t], down_y, RELAY),
+            send_rows(xv.at[pl.ds(far, half)], relay_buf.at[0, t], up_y, RELAY, half),
+            send_rows(xv.at[pl.ds(far + half, half)], relay_buf.at[1, t], down_y, RELAY, half),
         )
 
     def far_pass(t):
-        relay[t][0].wait_recv()
-        up = send(relay_buf.at[0, t], xfull.at[y_down, pl.ds(t * STEP, half)], up_y, PASSED)
-        relay[t][1].wait_recv()
-        down = send(relay_buf.at[1, t], xfull.at[y_up, pl.ds(t * STEP + half, half)], down_y, PASSED)
+        relay[t][0]()
+        up = send_rows(relay_buf.at[0, t], xfull.at[y_down, pl.ds(t * STEP, half)], up_y, PASSED, half)
+        relay[t][1]()
+        lands = xfull.at[y_up, pl.ds(t * STEP + half, half)]
+        down = send_rows(relay_buf.at[1, t], lands, down_y, PASSED, half)
         passed[t] = (up, down)
 
     def tiles(r, start, count):
@@ -135,43 +142,39 @@
 
         lax.fori_loop(0, QUARTER, pick, 0, unroll=True)
 
-        ref = tiles(r, dim * QUARTER, QUARTER)
-        y_copies[r] = [send(ref, ref, target, PICK + r) for target in (up_y, down_y, far_y)]
+        place = dim * QUARTER
+        y_copies[r] = [send_tiles(r, place, place, QUARTER, target, PICK) for target in (up_y, down_y, far_y)]
 
     def first_send(r):
-        for copy in y_copies[r]:
-            copy.wait_recv()
-        block = tiles(r, 0, BLOCK)
+        for landed in y_copies[r]:
+            landed()
         first[r] = [
-            send(block, tiles(r, k * BLOCK, BLOCK), target, FIRST + r)
+            send_tiles(r, 0, k * BLOCK, BLOCK, target, FIRST)
             for k, target in ((3, far_a), (1, up_a), (2, down_a))
         ]
 
     def second_send(r):
-        for copy in first[r]:
-            copy.wait_recv()
-        bundle = tiles(r, 0, BUNDLE)
+        for landed in first[r]:
+            landed()
         second[r] = (
-            send(bundle, tiles(r, BUNDLE, BUNDLE), up_b, SECOND + r),
-            send(bundle, tiles(r, 2 * BUNDLE, BUNDLE), down_b, SECOND + r),
-        )
-        swap[r] = [send(bundle, bundle, (sibling, dim), SWAP + r)]
+            send_tiles(r, 0, BUNDLE, BUNDLE, up_b, SECOND),
+            send_tiles(r, 0, 2 * BUNDLE, BUNDLE, down_b, SECOND),
+        )
+        swap[r] = [send_tiles(r, 0, 0, BUNDLE, (sibling, dim), SWAP)]
 
     def second_pass(r):
         part = 2 * BLOCK
-        second[r][0].wait_recv()
-        up = send(tiles(r, BUNDLE, part), tiles(r, 3 * BUNDLE, part), up_b, SECOND + r)
-        second[r][1].wait_recv()
-        down = send(tiles(r, 2 * BUNDLE + part, part), tiles(r, 3 * BUNDLE + part, part), down_b, SECOND + r)
+        second[r][0]()
+        up = send_tiles(r, BUNDLE, 3 * BUNDLE, part, up_b, SECOND)
+        second[r][1]()
+        down = send_tiles(r, 2 * BUNDLE + part, 3 * BUNDLE + part, part, down_b, SECOND)
         passes[r] = (up, down)
-        ready = tiles(r, BUNDLE, 2 * BUNDLE)
-        swap[r].append(send(ready, ready, (sibling, dim), SWAP + r))
+        swap[r].append(send_tiles(r, BUNDLE, BUNDLE, 2 * BUNDLE, (sibling, dim), SWAP))
 
     def second_end(r):
-        for copy in passes[r]:
-            copy.wait_recv()
-        ready = tiles(r, 3 * BUNDLE, BUNDLE)
-        swap[r].append(send(ready, ready, (sibling, dim), SWAP + r))
+        for landed in passes[r]:
+            landed()
+        swap[r].append(send_tiles(r, 3 * BUNDLE, 3 * BUNDLE, BUNDLE, (sibling, dim), SWAP))
 
     def convert(r, side, bundle, count=1):
         start = (core * HALF if side == 0 else (1 - core) * HALF) + bundle * BUNDLE
@@ -194,8 +197,8 @@
         lax.fori_loop(bundle, bundle + count, one, 0)
 
     def prepare(t):
-        for copy in near[t] + passed[t]:
-            copy.wait_recv()
+        for landed in near[t] + passed[t]:
+            landed()
         at = slice(t % 2 * STEP, (t % 2 + 1) * STEP)
         total = jnp.zeros((LANES, STEP), F32)
         for q in range(4):
@@ -228,16 +231,9 @@
             [jnp.maximum(value + norm, 0.0) for value in best], axis=0
         )
 
-    def many(count, body):
-        def one(k, carry):
-            body(k)
-            return carry
-
-        lax.fori_loop(0, count, one, 0)
-
     def convert_swapped(r):
-        for copy in swap[r]:
-            copy.wait_recv()
+        for landed in swap[r]:
+            landed()
         convert(r, 1, 0, 4)
 
     pick_send(0)
@@ -273,33 +269,51 @@
     convert(2, 0, 0)
     near_send(3)
     prepare(1)
-    nearest(0, 0, 0)
-    second_pass(2)
-    convert(2, 0, 1, 2)
-    second_end(1)
-    convert_swapped(0)
-    convert(1, 0, 3)
-    nearest(0, 0, 1)
-    second_end(2)
-    nearest(0, 1, 0)
-    convert(2, 0, 3)
-    convert_swapped(1)
-    nearest(0, 2, 0)
-    nearest(0, 1, 1)
-    prepare(2)
-    convert_swapped(2)
-    nearest(0, 2, 1)
-    finish(0)
-    for r in range(ROUNDS):
-        sent(cand[r].at[pl.ds(0, 3 * QUARTER)], PICK + r)
-        sent(cand[r].at[pl.ds(0, 3 * BLOCK)], FIRST + r)
-        sent(cand[r].at[pl.ds(0, 3 * BUNDLE)], SECOND + r)
-        sent(cand[r].at[pl.ds(0, HALF)], SWAP + r)
-    prepare(3)
-    sent(xfull.at[pl.ds(0, 1)], RELAY)
-    sent(xfull.at[pl.ds(0, 2)], NEAR)
-    sent(xfull.at[pl.ds(0, 1)], PASSED)
-    many(2 * ROUNDS, lambda k: nearest(1, k // 2, k % 2))
+
+    def product(k, carry):
+        @pl.when(k == 1)
+        def _():
+            second_pass(2)
+            convert(2, 0, 1, 2)
+            second_end(1)
+            convert_swapped(0)
+            convert(1, 0, 3)
+
+        @pl.when(k == 2)
+        def _():
+            second_end(2)
+
+        @pl.when(k == 3)
+        def _():
+            convert(2, 0, 3)
+            convert_swapped(1)
+
+        @pl.when(k == 5)
+        def _():
+            prepare(2)
+            convert_swapped(2)
+
+        @pl.when(k == 6)
+        def _():
+            finish(0)
+            for r in range(ROUNDS):
+                sent(cand[r].at[pl.ds(0, 3 * QUARTER)], PICK + r)
+                sent(cand[r].at[pl.ds(0, 3 * BLOCK)], FIRST + r)
+                sent(cand[r].at[pl.ds(0, 3 * BUNDLE)], SECOND + r)
+                sent(cand[r].at[pl.ds(0, HALF)], SWAP + r)
+            prepare(3)
+            sent(xfull.at[pl.ds(0, 1)], RELAY)
+            sent(xfull.at[pl.ds(0, 2)], NEAR)
+            sent(xfull.at[pl.ds(0, 1)], PASSED)
+
+        pair = jnp.where(k > 5, 1, 0)
+        m = k - 6 * pair
+        r = jnp.where(m < 2, 0, jnp.where((m == 2) | (m == 4), 1, 2))
+        side = jnp.where((m == 1) | (m > 3), 1, 0)
+        nearest(pair, r, side)
+        return carry
+
+    lax.fori_loop(0, 2 * 2 * ROUNDS, product, 0)
     finish(1)
 
     sums = sum([done[:, k * LANES:(k + 1) * LANES] for k in range(SHARE // LANES)])

time: 56.1 us -> 56.7 us (1.011)
  Pallas kernels: 54.6 us -> 55.2 us
    pallas_call x1, Pallas kernels: 54.6 us -> 55.2 us  [local(): pl.pallas_call(kernel, out_shape=jax.ShapeDtypeStruct((ROUNDS, SHARE), F3...]
where the time goes in v1:
time: 56.7 us; the launch traced here: 56.5 us
  Pallas kernels  55.2 us (97%)
  local copies, waits for them, and re-layouts  1.33 us (2%)
    pallas_call x1, Pallas kernels, local(): pl.pallas_call(kernel, out_shape=jax.ShapeDtypeStruct((ROUNDS, SHARE), F3...  55.2 us
    unnamed x1, local copies, waits for them, and re-layouts  1.33 us

profile of v1, /device:TPU:1, one launch (start us, length us, event | category | flops | bytes accessed | tf_op | source)
XLA Modules:
  0.0 56.5 jit_solution(10661104905196166102)
XLA Ops:
  0.0 55.2 %shard_map.37 = f32[3,1024]{1,0:T(4,128)} custom-call(s32[3,32]{1,0:T(4,128)} %index_hbm.1, s32[3,32]{1,0:T(4,128)} %count_hbm.1, f32[4096,128]{1,0:T(8,128)} %x_ref.1), custom_call_target="tpu_custom_call" | custom-call | tf_op jit(solution)/shard_map/pallas_call | solution.py:343
  55.2 1.3 %copy.5 = f32[3,1024]{1,0:T(4,128)} copy(f32[3,1024]{1,0:T(4,128)} %shard_map.37) | data formatting | bytes 24576

commit v2 on v0

--- a/solution.py
+++ b/solution.py
@@ -25,6 +25,7 @@
 BLOCK = 4 * QUARTER
 BUNDLE = 4 * BLOCK
 HALF = 4 * BUNDLE
+LOADS = 4
 CORE_SLOTS = 512
 BF16 = jnp.bfloat16
 F32 = jnp.float32
@@ -65,15 +66,17 @@
         line_devices += [(item, ys[k]), (sibling, ys[k])]
     plane_devices = [plane(dz, dx) for dz in range(4) for dx in range(4) if dz or dx]
 
-    loads = [
-        pltpu.make_async_copy(index_hbm, index_ref, load_sem.at[0]),
-        pltpu.make_async_copy(x_ref, xv, load_sem.at[1]),
-        pltpu.make_async_copy(count_hbm, count_ref, load_sem.at[2]),
-        pltpu.make_async_copy(x_ref.at[pl.ds(dim * SHARE, SHARE)], xfull.at[dim], load_sem.at[3]),
-    ]
-    for copy in loads:
+    index_load = pltpu.make_async_copy(index_hbm, index_ref, load_sem.at[0])
+    count_load = pltpu.make_async_copy(count_hbm, count_ref, load_sem.at[1])
+    x_loads = []
+    for k in range(LOADS):
+        at = pl.ds(k * (ROWS // LOADS), ROWS // LOADS)
+        x_loads.append(pltpu.make_async_copy(x_ref.at[at], xv.at[at], load_sem.at[3 + k]))
+    for copy in [index_load, count_load] + x_loads:
         copy.start()
-    index_load, x_load, count_load, own_rows = loads
+    own_rows = pltpu.make_async_copy(
+        x_ref.at[pl.ds(dim * SHARE, SHARE)], xfull.at[dim], load_sem.at[2]
+    )
 
     barrier = pltpu.get_barrier_semaphore()
     for target in line_devices + plane_devices:
@@ -81,7 +84,8 @@
 
     index_load.wait()
     count_load.wait()
-    x_load.wait()
+    for copy in x_loads:
+        copy.wait()
     pl.semaphore_wait(barrier, REDUCES)
 
     number = itertools.count()
@@ -136,7 +140,7 @@
         lax.fori_loop(0, QUARTER, pick, 0, unroll=True)
 
         ref = tiles(r, dim * QUARTER, QUARTER)
-        y_copies[r] = [send(ref, ref, target, PICK + r) for target in (up_y, down_y, far_y)]
+        y_copies[r] = [send(ref, ref, target, PICK + r) for target in (far_y, up_y, down_y)]
 
     def first_send(r):
         for copy in y_copies[r]:
@@ -150,12 +154,14 @@
     def second_send(r):
         for copy in first[r]:
             copy.wait_recv()
-        bundle = tiles(r, 0, BUNDLE)
-        second[r] = (
-            send(bundle, tiles(r, BUNDLE, BUNDLE), up_b, SECOND + r),
-            send(bundle, tiles(r, 2 * BUNDLE, BUNDLE), down_b, SECOND + r),
-        )
-        swap[r] = [send(bundle, bundle, (sibling, dim), SWAP + r)]
+        part = 2 * BLOCK
+
+        def send_part(start, to, target):
+            return send(tiles(r, start, part), tiles(r, to + start, part), target, SECOND + r)
+
+        second[r] = [send_part(0, BUNDLE, up_b), send_part(part, 2 * BUNDLE, down_b)]
+        second[r] += [send_part(part, BUNDLE, up_b), send_part(0, 2 * BUNDLE, down_b)]
+        swap[r] = [send(tiles(r, 0, BUNDLE), tiles(r, 0, BUNDLE), (sibling, dim), SWAP + r)]
 
     def second_pass(r):
         part = 2 * BLOCK
@@ -164,6 +170,8 @@
         second[r][1].wait_recv()
         down = send(tiles(r, 2 * BUNDLE + part, part), tiles(r, 3 * BUNDLE + part, part), down_b, SECOND + r)
         passes[r] = (up, down)
+        for copy in second[r][2:]:
+            copy.wait_recv()
         ready = tiles(r, BUNDLE, 2 * BUNDLE)
         swap[r].append(send(ready, ready, (sibling, dim), SWAP + r))
 
@@ -242,6 +250,7 @@
 
     pick_send(0)
     pick_send(1)
+    own_rows.start()
     far_send(0)
     pick_send(2)
     first_send(0)
@@ -319,7 +328,7 @@
     sent(red_plane, COST + 1)
 
 
-COPIES = ROUNDS * 13 + PIECES * 6
+COPIES = ROUNDS * 15 + PIECES * 6
 REDUCES = 22
 PICK, FIRST, SECOND, SWAP, RELAY, NEAR, PASSED, COST = 0, 3, 6, 9, 12, 13, 14, 15
 ANY = pl.BlockSpec(memory_space=pl.ANY)
@@ -349,7 +358,7 @@
             pltpu.VMEM((2, 8, LANES), F32),
             pltpu.VMEM((7, 8, LANES), F32),
             pltpu.VMEM((15, 8, LANES), F32),
-            pltpu.SemaphoreType.DMA((4,)),
+            pltpu.SemaphoreType.DMA((3 + LOADS,)),
             pltpu.SemaphoreType.DMA((COST + 2,)),
             pltpu.SemaphoreType.DMA((COPIES,)),
             pltpu.SemaphoreType.DMA((2,)),

time: 56.1 us -> 54.9 us (0.979)
  Pallas kernels: 54.6 us -> 53.3 us
    pallas_call x1, Pallas kernels: 54.6 us -> 53.3 us  [local(): pl.pallas_call(kernel, out_shape=jax.ShapeDtypeStruct((ROUNDS, SHARE), F3...]
where the time goes in v2:
time: 54.9 us; the launch traced here: 54.7 us
  Pallas kernels  53.3 us (97%)
  local copies, waits for them, and re-layouts  1.33 us (2%)
    pallas_call x1, Pallas kernels, local(): pl.pallas_call(kernel, out_shape=jax.ShapeDtypeStruct((ROUNDS, SHARE), F3...  53.3 us
    unnamed x1, local copies, waits for them, and re-layouts  1.33 us

profile of v2, /device:TPU:1, one launch (start us, length us, event | category | flops | bytes accessed | tf_op | source)
XLA Modules:
  0.0 54.7 jit_solution(1532513317630140793)
XLA Ops:
  0.0 53.3 %shard_map.37 = f32[3,1024]{1,0:T(4,128)} custom-call(s32[3,32]{1,0:T(4,128)} %index_hbm.1, s32[3,32]{1,0:T(4,128)} %count_hbm.1, f32[4096,128]{1,0:T(8,128)} %x_ref.1), custom_call_target="tpu_custom_call" | custom-call | tf_op jit(solution)/shard_map/pallas_call | solution.py:338
  53.3 1.3 %copy.5 = f32[3,1024]{1,0:T(4,128)} copy(f32[3,1024]{1,0:T(4,128)} %shard_map.37) | data formatting | bytes 24576

commit v3 on v2

--- a/solution.py
+++ b/solution.py
@@ -176,10 +176,11 @@
         swap[r].append(send(ready, ready, (sibling, dim), SWAP + r))
 
     def second_end(r):
-        for copy in passes[r]:
-            copy.wait_recv()
-        ready = tiles(r, 3 * BUNDLE, BUNDLE)
-        swap[r].append(send(ready, ready, (sibling, dim), SWAP + r))
+        part = 2 * BLOCK
+        for k, copy in enumerate(passes[r]):
+            copy.wait_recv()
+            ready = tiles(r, 3 * BUNDLE + k * part, part)
+            swap[r].append(send(ready, ready, (sibling, dim), SWAP + r))
 
     def convert(r, side, bundle, count=1):
         start = (core * HALF if side == 0 else (1 - core) * HALF) + bundle * BUNDLE
@@ -243,10 +244,10 @@
 
         lax.fori_loop(0, count, one, 0)
 
-    def convert_swapped(r):
-        for copy in swap[r]:
-            copy.wait_recv()
-        convert(r, 1, 0, 4)
+    def other(r, step):
+        for copy in (swap[r][0:1], swap[r][1:2], swap[r][2:4])[step]:
+            copy.wait_recv()
+        convert(r, 1, (0, 1, 3)[step], (1, 2, 1)[step])
 
     pick_send(0)
     pick_send(1)
@@ -269,9 +270,11 @@
     far_pass(1)
     own_rows.wait()
     prepare(0)
+    other(0, 0)
     second_pass(0)
     convert(0, 0, 1, 2)
     second_send(2)
+    other(1, 0)
     second_pass(1)
     convert(1, 0, 1, 2)
     near_send(2)
@@ -280,23 +283,27 @@
     far_pass(3)
     convert(0, 0, 3)
     convert(2, 0, 0)
+    other(0, 1)
     near_send(3)
     prepare(1)
     nearest(0, 0, 0)
     second_pass(2)
     convert(2, 0, 1, 2)
     second_end(1)
-    convert_swapped(0)
+    other(0, 2)
+    nearest(0, 0, 1)
     convert(1, 0, 3)
-    nearest(0, 0, 1)
+    other(1, 1)
+    nearest(0, 1, 0)
     second_end(2)
-    nearest(0, 1, 0)
     convert(2, 0, 3)
-    convert_swapped(1)
+    other(1, 2)
+    other(2, 0)
     nearest(0, 2, 0)
     nearest(0, 1, 1)
+    other(2, 1)
     prepare(2)
-    convert_swapped(2)
+    other(2, 2)
     nearest(0, 2, 1)
     finish(0)
     for r in range(ROUNDS):
@@ -328,7 +335,7 @@
     sent(red_plane, COST + 1)
 
 
-COPIES = ROUNDS * 15 + PIECES * 6
+COPIES = ROUNDS * 16 + PIECES * 6
 REDUCES = 22
 PICK, FIRST, SECOND, SWAP, RELAY, NEAR, PASSED, COST = 0, 3, 6, 9, 12, 13, 14, 15
 ANY = pl.BlockSpec(memory_space=pl.ANY)

time: 54.9 us -> 54 us (0.984)
  Pallas kernels: 53.3 us -> 52.5 us
    pallas_call x1, Pallas kernels: 53.3 us -> 52.5 us  [local(): pl.pallas_call(kernel, out_shape=jax.ShapeDtypeStruct((ROUNDS, SHARE), F3...]
where the time goes in v3:
time: 54 us; the launch traced here: 53.8 us
  Pallas kernels  52.5 us (97%)
  local copies, waits for them, and re-layouts  1.33 us (2%)
    pallas_call x1, Pallas kernels, local(): pl.pallas_call(kernel, out_shape=jax.ShapeDtypeStruct((ROUNDS, SHARE), F3...  52.5 us
    unnamed x1, local copies, waits for them, and re-layouts  1.33 us

profile of v3, /device:TPU:1, one launch (start us, length us, event | category | flops | bytes accessed | tf_op | source)
XLA Modules:
  0.0 53.8 jit_solution(13847543104382256676)
XLA Ops:
  0.0 52.5 %shard_map.37 = f32[3,1024]{1,0:T(4,128)} custom-call(s32[3,32]{1,0:T(4,128)} %index_hbm.1, s32[3,32]{1,0:T(4,128)} %count_hbm.1, f32[4096,128]{1,0:T(8,128)} %x_ref.1), custom_call_target="tpu_custom_call" | custom-call | tf_op jit(solution)/shard_map/pallas_call | solution.py:345
  52.5 1.3 %copy.5 = f32[3,1024]{1,0:T(4,128)} copy(f32[3,1024]{1,0:T(4,128)} %shard_map.37) | data formatting | bytes 24576

commit v4 on v3

--- a/solution.py
+++ b/solution.py
@@ -79,14 +79,15 @@
     )
 
     barrier = pltpu.get_barrier_semaphore()
-    for target in line_devices + plane_devices:
+    near_devices = [far_y, up_y, down_y, far_a, up_a, down_a, up_b, down_b, (sibling, dim)]
+    for target in near_devices:
         pl.semaphore_signal(barrier, inc=1, device_id=target, device_id_type=MESH)
 
     index_load.wait()
     count_load.wait()
     for copy in x_loads:
         copy.wait()
-    pl.semaphore_wait(barrier, REDUCES)
+    pl.semaphore_wait(barrier, len(near_devices))
 
     number = itertools.count()
 
@@ -336,7 +337,6 @@
 
 
 COPIES = ROUNDS * 16 + PIECES * 6
-REDUCES = 22
 PICK, FIRST, SECOND, SWAP, RELAY, NEAR, PASSED, COST = 0, 3, 6, 9, 12, 13, 14, 15
 ANY = pl.BlockSpec(memory_space=pl.ANY)
 

time: 54 us -> 53.6 us (level)
  no operation moved by 1% of the time
where the time goes in v4:
time: 53.6 us; the launch traced here: 53.4 us
  Pallas kernels  52.1 us (97%)
  local copies, waits for them, and re-layouts  1.33 us (2%)
    pallas_call x1, Pallas kernels, local(): pl.pallas_call(kernel, out_shape=jax.ShapeDtypeStruct((ROUNDS, SHARE), F3...  52.1 us
    unnamed x1, local copies, waits for them, and re-layouts  1.33 us

profile of v4, /device:TPU:1, one launch (start us, length us, event | category | flops | bytes accessed | tf_op | source)
XLA Modules:
  0.0 53.4 jit_solution(16293932491840700993)
XLA Ops:
  0.0 52.1 %shard_map.37 = f32[3,1024]{1,0:T(4,128)} custom-call(s32[3,32]{1,0:T(4,128)} %index_hbm.1, s32[3,32]{1,0:T(4,128)} %count_hbm.1, f32[4096,128]{1,0:T(8,128)} %x_ref.1), custom_call_target="tpu_custom_call" | custom-call | tf_op jit(solution)/shard_map/pallas_call | solution.py:345
  52.1 1.3 %copy.5 = f32[3,1024]{1,0:T(4,128)} copy(f32[3,1024]{1,0:T(4,128)} %shard_map.37) | data formatting | bytes 24576

commit v5 on v4

--- a/solution.py
+++ b/solution.py
@@ -226,6 +226,19 @@
         )
         value = value + jnp.concatenate([nrm[r, side]] * (WIDE // LANES), axis=1)
         low[t, r, side] = jnp.min(value.reshape(CORE_SLOTS // 8, 8, WIDE), axis=0)
+
+    def nearest_both(t, r):
+        high, rows = ch[r].reshape(2 * CORE_SLOTS, 512), xh[t]
+        value = jnp.dot(
+            jnp.concatenate([high, cl[r].reshape(2 * CORE_SLOTS, 512), high], axis=1),
+            jnp.concatenate([rows, rows, xl[t]], axis=0),
+            preferred_element_type=F32,
+        )
+        norm = nrm[r].reshape(2 * CORE_SLOTS, LANES)
+        value = value + jnp.concatenate([norm] * (WIDE // LANES), axis=1)
+        value = jnp.min(value.reshape(2 * CORE_SLOTS // 8, 8, WIDE), axis=0)
+        low[t, r, 0] = value
+        low[t, r, 1] = value
 
     def finish(t):
         norm = jnp.sum(sq[t], axis=0, keepdims=True)
@@ -300,12 +313,11 @@
     convert(2, 0, 3)
     other(1, 2)
     other(2, 0)
-    nearest(0, 2, 0)
     nearest(0, 1, 1)
     other(2, 1)
     prepare(2)
     other(2, 2)
-    nearest(0, 2, 1)
+    nearest_both(0, 2)
     finish(0)
     for r in range(ROUNDS):
         sent(cand[r].at[pl.ds(0, 3 * QUARTER)], PICK + r)
@@ -316,7 +328,7 @@
     sent(xfull.at[pl.ds(0, 1)], RELAY)
     sent(xfull.at[pl.ds(0, 2)], NEAR)
     sent(xfull.at[pl.ds(0, 1)], PASSED)
-    many(2 * ROUNDS, lambda k: nearest(1, k // 2, k % 2))
+    many(ROUNDS, lambda r: nearest_both(1, r))
     finish(1)
 
     sums = sum([done[:, k * LANES:(k + 1) * LANES] for k in range(SHARE // LANES)])

time: 53.6 us -> 53.1 us (level)
  Pallas kernels: 52.1 us -> 51.5 us
    pallas_call x1, Pallas kernels: 52.1 us -> 51.5 us  [local(): pl.pallas_call(kernel, out_shape=jax.ShapeDtypeStruct((ROUNDS, SHARE), F3...]
where the time goes in v5:
time: 53.1 us; the launch traced here: 52.8 us
  Pallas kernels  51.5 us (97%)
  local copies, waits for them, and re-layouts  1.33 us (3%)
    pallas_call x1, Pallas kernels, local(): pl.pallas_call(kernel, out_shape=jax.ShapeDtypeStruct((ROUNDS, SHARE), F3...  51.5 us
    unnamed x1, local copies, waits for them, and re-layouts  1.33 us

profile of v5, /device:TPU:1, one launch (start us, length us, event | category | flops | bytes accessed | tf_op | source)
XLA Modules:
  0.0 52.8 jit_solution(13943264209837529518)
XLA Ops:
  0.0 51.5 %shard_map.37 = f32[3,1024]{1,0:T(4,128)} custom-call(s32[3,32]{1,0:T(4,128)} %index_hbm.1, s32[3,32]{1,0:T(4,128)} %count_hbm.1, f32[4096,128]{1,0:T(8,128)} %x_ref.1), custom_call_target="tpu_custom_call" | custom-call | tf_op jit(solution)/shard_map/pallas_call | solution.py:357
  51.5 1.3 %copy.5 = f32[3,1024]{1,0:T(4,128)} copy(f32[3,1024]{1,0:T(4,128)} %shard_map.37) | data formatting | bytes 24576

commit v6 on v5

--- a/solution.py
+++ b/solution.py
@@ -262,6 +262,16 @@
         for copy in (swap[r][0:1], swap[r][1:2], swap[r][2:4])[step]:
             copy.wait_recv()
         convert(r, 1, (0, 1, 3)[step], (1, 2, 1)[step])
+
+    def all_sent():
+        for r in range(ROUNDS):
+            sent(cand[r].at[pl.ds(0, 3 * QUARTER)], PICK + r)
+            sent(cand[r].at[pl.ds(0, 3 * BLOCK)], FIRST + r)
+            sent(cand[r].at[pl.ds(0, 3 * BUNDLE)], SECOND + r)
+            sent(cand[r].at[pl.ds(0, HALF)], SWAP + r)
+        sent(xfull.at[pl.ds(0, 1)], RELAY)
+        sent(xfull.at[pl.ds(0, 2)], NEAR)
+        sent(xfull.at[pl.ds(0, 1)], PASSED)
 
     pick_send(0)
     pick_send(1)
@@ -319,15 +329,7 @@
     other(2, 2)
     nearest_both(0, 2)
     finish(0)
-    for r in range(ROUNDS):
-        sent(cand[r].at[pl.ds(0, 3 * QUARTER)], PICK + r)
-        sent(cand[r].at[pl.ds(0, 3 * BLOCK)], FIRST + r)
-        sent(cand[r].at[pl.ds(0, 3 * BUNDLE)], SECOND + r)
-        sent(cand[r].at[pl.ds(0, HALF)], SWAP + r)
     prepare(3)
-    sent(xfull.at[pl.ds(0, 1)], RELAY)
-    sent(xfull.at[pl.ds(0, 2)], NEAR)
-    sent(xfull.at[pl.ds(0, 1)], PASSED)
     many(ROUNDS, lambda r: nearest_both(1, r))
     finish(1)
 
@@ -340,6 +342,8 @@
                 src_ref=part.at[stage], dst_ref=landed.at[k], send_sem=send_sem.at[COST + stage],
                 recv_sem=cost_sem.at[stage], device_id=target, device_id_type=MESH,
             ).start()
+        if stage == 0:
+            all_sent()
         pltpu.make_async_copy(landed, landed, cost_sem.at[stage]).wait()
         line = line + jnp.sum(landed[...], axis=0)
     cost = jnp.sum(line, axis=1, keepdims=True)[:ROUNDS]

time: 53.1 us -> 53 us (level)
  no operation moved by 1% of the time
where the time goes in v6:
time: 53 us; the launch traced here: 52.8 us
  Pallas kernels  51.5 us (97%)
  local copies, waits for them, and re-layouts  1.33 us (3%)
    pallas_call x1, Pallas kernels, local(): pl.pallas_call(kernel, out_shape=jax.ShapeDtypeStruct((ROUNDS, SHARE), F3...  51.5 us
    unnamed x1, local copies, waits for them, and re-layouts  1.33 us

profile of v6, /device:TPU:1, one launch (start us, length us, event | category | flops | bytes accessed | tf_op | source)
XLA Modules:
  0.0 52.8 jit_solution(15225305585884333231)
XLA Ops:
  0.0 51.5 %shard_map.37 = f32[3,1024]{1,0:T(4,128)} custom-call(s32[3,32]{1,0:T(4,128)} %index_hbm.1, s32[3,32]{1,0:T(4,128)} %count_hbm.1, f32[4096,128]{1,0:T(8,128)} %x_ref.1), custom_call_target="tpu_custom_call" | custom-call | tf_op jit(solution)/shard_map/pallas_call | solution.py:361
  51.5 1.3 %copy.5 = f32[3,1024]{1,0:T(4,128)} copy(f32[3,1024]{1,0:T(4,128)} %shard_map.37) | data formatting | bytes 24576

commit v7 on v6

--- a/solution.py
+++ b/solution.py
@@ -274,56 +274,56 @@
         sent(xfull.at[pl.ds(0, 1)], PASSED)
 
     pick_send(0)
+    far_send(0)
     pick_send(1)
     own_rows.start()
-    far_send(0)
-    pick_send(2)
+    near_send(0)
     first_send(0)
     far_send(1)
+    far_send(2)
     first_send(1)
-    near_send(0)
-    first_send(2)
     second_send(0)
+    pick_send(2)
     far_pass(0)
-    convert(0, 0, 0)
     second_send(1)
-    far_send(2)
     convert(1, 0, 0)
     near_send(1)
-    far_send(3)
+    convert(0, 0, 0)
+    first_send(2)
+    other(0, 0)
+    second_pass(0)
     far_pass(1)
+    convert(0, 0, 1, 2)
     own_rows.wait()
     prepare(0)
-    other(0, 0)
-    second_pass(0)
-    convert(0, 0, 1, 2)
-    second_send(2)
+    far_pass(2)
+    far_send(3)
+    near_send(2)
     other(1, 0)
     second_pass(1)
+    second_send(2)
     convert(1, 0, 1, 2)
-    near_send(2)
-    far_pass(2)
+    convert(2, 0, 0)
     second_end(0)
-    far_pass(3)
     convert(0, 0, 3)
-    convert(2, 0, 0)
     other(0, 1)
     near_send(3)
     prepare(1)
     nearest(0, 0, 0)
-    second_pass(2)
-    convert(2, 0, 1, 2)
     second_end(1)
     other(0, 2)
     nearest(0, 0, 1)
+    second_pass(2)
+    far_pass(3)
+    convert(2, 0, 1, 2)
     convert(1, 0, 3)
     other(1, 1)
+    other(2, 0)
     nearest(0, 1, 0)
+    other(1, 2)
+    nearest(0, 1, 1)
     second_end(2)
     convert(2, 0, 3)
-    other(1, 2)
-    other(2, 0)
-    nearest(0, 1, 1)
     other(2, 1)
     prepare(2)
     other(2, 2)

time: 53 us -> 54.3 us (1.025)
  Pallas kernels: 51.5 us -> 52.8 us
    pallas_call x1, Pallas kernels: 51.5 us -> 52.8 us  [local(): pl.pallas_call(kernel, out_shape=jax.ShapeDtypeStruct((ROUNDS, SHARE), F3...]
where the time goes in v7:
time: 54.3 us; the launch traced here: 54.1 us
  Pallas kernels  52.8 us (97%)
  local copies, waits for them, and re-layouts  1.33 us (2%)
    pallas_call x1, Pallas kernels, local(): pl.pallas_call(kernel, out_shape=jax.ShapeDtypeStruct((ROUNDS, SHARE), F3...  52.8 us
    unnamed x1, local copies, waits for them, and re-layouts  1.33 us

profile of v7, /device:TPU:1, one launch (start us, length us, event | category | flops | bytes accessed | tf_op | source)
XLA Modules:
  0.0 54.1 jit_solution(10236339488288457253)
XLA Ops:
  0.0 52.8 %shard_map.37 = f32[3,1024]{1,0:T(4,128)} custom-call(s32[3,32]{1,0:T(4,128)} %index_hbm.1, s32[3,32]{1,0:T(4,128)} %count_hbm.1, f32[4096,128]{1,0:T(8,128)} %x_ref.1), custom_call_target="tpu_custom_call" | custom-call | tf_op jit(solution)/shard_map/pallas_call | solution.py:361
  52.8 1.3 %copy.5 = f32[3,1024]{1,0:T(4,128)} copy(f32[3,1024]{1,0:T(4,128)} %shard_map.37) | data formatting | bytes 24576

commit v8 on v6

--- a/solution.py
+++ b/solution.py
@@ -296,8 +296,8 @@
     prepare(0)
     other(0, 0)
     second_pass(0)
+    second_send(2)
     convert(0, 0, 1, 2)
-    second_send(2)
     other(1, 0)
     second_pass(1)
     convert(1, 0, 1, 2)
@@ -310,8 +310,8 @@
     other(0, 1)
     near_send(3)
     prepare(1)
+    second_pass(2)
     nearest(0, 0, 0)
-    second_pass(2)
     convert(2, 0, 1, 2)
     second_end(1)
     other(0, 2)

time: 53 us -> 53 us (level)
  no operation moved by 1% of the time
where the time goes in v8:
time: 53 us; the launch traced here: 52.8 us
  Pallas kernels  51.5 us (97%)
  local copies, waits for them, and re-layouts  1.33 us (3%)
    pallas_call x1, Pallas kernels, local(): pl.pallas_call(kernel, out_shape=jax.ShapeDtypeStruct((ROUNDS, SHARE), F3...  51.5 us
    unnamed x1, local copies, waits for them, and re-layouts  1.33 us

profile of v8, /device:TPU:1, one launch (start us, length us, event | category | flops | bytes accessed | tf_op | source)
XLA Modules:
  0.0 52.8 jit_solution(13719965413388493339)
XLA Ops:
  0.0 51.5 %shard_map.37 = f32[3,1024]{1,0:T(4,128)} custom-call(s32[3,32]{1,0:T(4,128)} %index_hbm.1, s32[3,32]{1,0:T(4,128)} %count_hbm.1, f32[4096,128]{1,0:T(8,128)} %x_ref.1), custom_call_target="tpu_custom_call" | custom-call | tf_op jit(solution)/shard_map/pallas_call | solution.py:361
  51.5 1.3 %copy.5 = f32[3,1024]{1,0:T(4,128)} copy(f32[3,1024]{1,0:T(4,128)} %shard_map.37) | data formatting | bytes 24576

commit v9 on v8

--- a/solution.py
+++ b/solution.py
@@ -318,14 +318,13 @@
     nearest(0, 0, 1)
     convert(1, 0, 3)
     other(1, 1)
-    nearest(0, 1, 0)
+    other(2, 0)
+    prepare(2)
     second_end(2)
     convert(2, 0, 3)
     other(1, 2)
-    other(2, 0)
-    nearest(0, 1, 1)
+    nearest_both(0, 1)
     other(2, 1)
-    prepare(2)
     other(2, 2)
     nearest_both(0, 2)
     finish(0)

time: 53 us -> 53.4 us (level)
  no operation moved by 1% of the time
where the time goes in v9:
time: 53.4 us; the launch traced here: 53.2 us
  Pallas kernels  51.9 us (97%)
  local copies, waits for them, and re-layouts  1.33 us (2%)
    pallas_call x1, Pallas kernels, local(): pl.pallas_call(kernel, out_shape=jax.ShapeDtypeStruct((ROUNDS, SHARE), F3...  51.9 us
    unnamed x1, local copies, waits for them, and re-layouts  1.33 us

profile of v9, /device:TPU:1, one launch (start us, length us, event | category | flops | bytes accessed | tf_op | source)
XLA Modules:
  0.0 53.2 jit_solution(8151593217492973217)
XLA Ops:
  0.0 51.9 %shard_map.37 = f32[3,1024]{1,0:T(4,128)} custom-call(s32[3,32]{1,0:T(4,128)} %index_hbm.1, s32[3,32]{1,0:T(4,128)} %count_hbm.1, f32[4096,128]{1,0:T(8,128)} %x_ref.1), custom_call_target="tpu_custom_call" | custom-call | tf_op jit(solution)/shard_map/pallas_call | solution.py:360
  51.9 1.3 %copy.5 = f32[3,1024]{1,0:T(4,128)} copy(f32[3,1024]{1,0:T(4,128)} %shard_map.37) | data formatting | bytes 24576
